TPU v7x, 256 devices: a whole 4x4x8 slice. The times are simulated.
256 devices in a mesh: cuts: 16 (over x, y), det: 2 (over core), bank: 8 (over z).
Axes of the slice: x: 4, y: 4, z: 8, core: 2. Of those that a mesh axis runs over, the one named last changes fastest.
Arguments:
- strain: bfloat16 [16, 2, 6144], P('cuts', 'det'), may hold values from -6 to 6
- filters: bfloat16 [128, 256, 2048], P(('bank', 'cuts')), parts along dimension 0, may hold values from -0.125 to 0.125
- recon_weights: bfloat16 [128, 512, 256], P(('bank', 'cuts')), parts along dimension 0, may hold values from -0.09375 to 0.09375
- row_spans: int32 [4096], P('bank'), parts along dimension 0, may hold values from 1 to 16
- slice_rates: int32 [16], replicated, may hold values from 1 to 8, as said below
- delays: int32 [64, 2], replicated, may hold values from 0 to 47
- antenna: float32 [64, 2], replicated, may hold values from 0.2 to 1
Outputs:
- peak_amplitude: float32 [4096, 4096], P(('bank', 'cuts', 'det')), parts along dimension 0
There are 8 independent parts, one for each index of `bank`. A program takes and returns all parts, laid end to end along the dimension named above; an argument that names none is the same for every part. Nothing has to cross between parts.
Inputs may be any that keep to these rules, and one draw needn't show every extreme that they name: `slice_rates`: every entry is a power of two; entries never fall along the slices; the first is 1 and the last is 8.
All inputs are finite; a program needn't handle non-finite values.
Results may differ from a plain program's by a relative error of at most 0.0014.
Values sent between devices are 32-bit elements; how exact they have to be, the bound alone decides.
No kernel may reach another device: no remote copies, remote signals or barrier semaphores. Data moves between devices by JAX's collectives and lax.ppermute only.
A program may use at most 64 MiB of HBM per device.

v0:
```python
import jax
import jax.numpy as jnp
from jax import lax
from jax.sharding import PartitionSpec as P

BLOCK = 512
MAXD = 48


def hankel_block(segment, block_rows, tap_count):
    backward = jnp.concatenate([segment[::-1], jnp.zeros((1,), segment.dtype)])
    length = backward.shape[0]
    tiled = jnp.tile(backward, block_rows + 1)[: block_rows * (length - 1)]
    return tiled.reshape(block_rows, length - 1)[:, block_rows - 1 : block_rows - 1 + tap_count]


def filter_slice(samples, taps_bank, live_count, block_rows):
    tap_count = taps_bank.shape[1]
    window = samples.shape[0] - tap_count

    def one_block(block_index, output):
        offset = block_index * block_rows
        segment = lax.dynamic_slice_in_dim(samples, offset + 1, block_rows + tap_count - 1, 0)
        toeplitz = hankel_block(segment, block_rows, tap_count)
        result_block = jnp.einsum(
            "bt,it->bi", taps_bank, toeplitz, preferred_element_type=jnp.float32
        )
        return lax.dynamic_update_slice_in_dim(output, result_block.astype(jnp.bfloat16), offset, 1)

    initial = jnp.zeros((taps_bank.shape[0], window), jnp.bfloat16)
    return lax.fori_loop(0, live_count, one_block, initial)


def coherent(series, delays, antenna):
    detectors, height, window = series.shape
    padded = jnp.concatenate([series, jnp.zeros((detectors, height, MAXD), series.dtype)], axis=2)

    def direction(number, highest):
        summed = jnp.zeros((height, window), jnp.float32)
        for detector in range(detectors):
            shifted = lax.dynamic_slice_in_dim(
                padded[detector], delays[number, detector], window, 1
            )
            summed = summed + antenna[number, detector] * shifted
        return jnp.maximum(highest, jnp.abs(summed))

    return lax.fori_loop(0, delays.shape[0], direction, jnp.zeros((height, window), jnp.float32))


def shards(strain, filters, recon_weights, row_spans, slice_rates, delays, antenna):
    slice_index = lax.axis_index("cuts")
    slices = lax.axis_size("cuts")
    factor = slice_rates[slice_index]
    samples = strain[0, 0]
    taps_bank = filters[0]
    window = samples.shape[0] - taps_bank.shape[1]
    live_count = window // BLOCK
    filtered = filter_slice(samples, taps_bank, live_count, BLOCK)
    weights = recon_weights[0]
    row_share = weights.shape[0] // slices
    moments = jnp.arange(window, dtype=jnp.int32)
    keeping = (slice_index < row_spans).astype(jnp.float32)
    product = jnp.dot(weights, filtered, preferred_element_type=jnp.float32) * keeping[:, None]
    combined = lax.psum_scatter(
        jnp.take(product, moments // factor, axis=1), "cuts", scatter_dimension=0, tiled=True
    )
    detector_rows = lax.all_to_all(
        combined.reshape(1, row_share, window), "det", split_axis=1, concat_axis=0, tiled=True
    )
    return coherent(detector_rows, delays, antenna)


def solution(mesh):
    placed = (
        P("cuts", "det", None),
        P(("bank", "cuts"), None, None),
        P(("bank", "cuts"), None, None),
        P("bank"),
        P(),
        P(),
        P(),
    )
    return jax.shard_map(
        shards,
        mesh=mesh,
        in_specs=placed,
        out_specs=P(("bank", "cuts", "det"), None),
        check_vma=False,
    )
```

profile of v0, /device:TPU:1, one launch (start us, length us, event | category | flops | bytes accessed | tf_op | source)
XLA Modules:
  0.0 733.1 jit_solution(9470707328443454362)
XLA Ops:
  8.6 2.0 compare_select_fusion
  14.5 127.2 %while.29 = (s32[]{:T(128)}, bf16[256,4096]{0,1:T(8,128)(2,1)}, bf16[6144]{0:T(1024)(128)(2,1)S(1)}, bf16[256,2048]{1,0:T(8,128)(2,1)}, s32[]{:T(128)}, /*index=...) while((s32[]{:T(128)}, bf16[256,4096]{0,1:T(8,128)(2,1)}, ...), condition=%wide.region_1.0_spmd, body=%wide.region_0.0_spmd.sunk | while | flops 537012224 | bytes 24437976 | solution.py:31
  15.0 4.6 tile.32
  19.6 1.7 slice-done
  21.3 5.5 reshape.91
  26.8 3.6 fusion.22
  30.9 4.6 tile.32
  35.5 1.7 slice-done
  37.2 5.5 reshape.91
  42.7 3.5 fusion.22
  46.8 4.6 tile.32
  51.4 1.7 slice-done
  53.1 5.5 reshape.91
  58.7 3.6 fusion.22
  62.7 4.6 tile.32
  67.3 1.7 slice-done
  69.1 5.5 reshape.91
  74.6 3.5 fusion.22
  78.6 4.6 tile.32
  83.2 1.7 slice-done
  85.0 5.5 reshape.91
  90.5 3.5 fusion.22
  94.5 4.6 tile.32
  99.1 1.7 slice-done
  100.8 5.5 reshape.91
  106.4 3.5 fusion.22
  110.4 4.6 tile.32
  115.0 1.7 slice-done
  116.7 5.5 reshape.91
  122.3 3.5 fusion.22
  126.3 4.6 tile.32
  130.9 1.7 slice-done
  132.6 5.5 reshape.91
  138.2 3.5 fusion.22
  141.7 6.1 multiply_bitcast_fusion
  147.8 21.4 %gather_fusion = f32[4096,512]{1,0:T(8,128)} fusion(f32[512,4096]{0,1:T(8,128)} %multiply_bitcast_fusion, s32[4096]{0:T(1024)S(1)} %broadcast_clamp_fusion), kind=kCustom, calls=%fused_computation | custom fusion | bytes 16793600 | tf_op jit(solution)/shard_map/jit(_take)/gather | solution.py:65
  169.3 5.8 select_bitcast_fusion
  175.1 9.0 %copy.11 = f32[512,4096]{1,0:T(8,128)} copy(f32[512,4096]{0,1:T(8,128)} %select_bitcast_fusion) | data formatting | bytes 16777216
  184.1 92.6 %reduce-scatter.4.cloned.1.call-done = f32[32,4096]{1,0:T(8,128)} async-done(((f32[512,4096]{1,0:T(8,128)}), f32[32,4096]{1,0:T(8,128)}) %reduce-scatter.4.cloned.1.call-update) | async-done | bytes 524304
  276.7 1.6 copy.12
  279.2 5.9 all_to_all.12
  285.5 440.0 %while.30 = (s32[]{:T(128)}, f32[16,4096]{1,0:T(8,128)S(1)}, f32[64,2]{0,1:T(2,128)S(1)}, f32[2,16,4144]{2,1,0:T(8,128)S(1)}, s32[64,2]{0,1:T(2,128)S(1)}, /*index=5*/s32[]{:T(128)}, s32[]{:T(128)}, s32[]{:T(128)}) while((s32[]{:T(128)}, f32[16,4096]{1,0:T(8,128)S(1)}, f32[64,2]{0,1:T(2,128)S(1)}, f32[2,16,4144]{2,1,0:T(8,128)S(1)}, ...), condition=%wide.region_4.5_spmd.clone, body=%wide.region_3.4_spmd.clone.sunk | while | flops 393225 | bytes 2109659 | solution.py:47
  304.6 1.6 bitcast_maximum_fusion.2
  311.4 1.6 bitcast_maximum_fusion.2
  318.3 1.6 bitcast_maximum_fusion.2
  345.8 1.6 bitcast_maximum_fusion.2
  352.7 1.6 bitcast_maximum_fusion.2
  359.6 1.6 bitcast_maximum_fusion.2
  387.1 1.6 bitcast_maximum_fusion.2
  393.9 1.6 bitcast_maximum_fusion.2
  400.8 1.6 bitcast_maximum_fusion.2
  407.7 1.6 bitcast_maximum_fusion.2
  435.2 1.6 bitcast_maximum_fusion.2
  442.1 1.6 bitcast_maximum_fusion.2
  448.9 1.6 bitcast_maximum_fusion.2
  476.4 1.6 bitcast_maximum_fusion.2
  483.3 1.6 bitcast_maximum_fusion.2
  490.2 1.6 bitcast_maximum_fusion.2
  517.7 1.6 bitcast_maximum_fusion.2
  524.6 1.6 bitcast_maximum_fusion.2
  531.5 1.6 bitcast_maximum_fusion.2
  538.3 1.6 bitcast_maximum_fusion.2
  565.8 1.6 bitcast_maximum_fusion.2
  572.7 1.6 bitcast_maximum_fusion.2
  (302 shorter events, 163.8 us)
Async XLA Ops:
  6.5 135.2 %copy-start = (bf16[1,512,256]{2,1,0:T(8,128)(2,1)S(1)}, bf16[1,512,256]{2,1,0:T(8,128)(2,1)}, u32[]{:S(2)}) copy-start(bf16[1,512,256]{2,1,0:T(8,128)(2,1)} %param.13) | copy-start | bytes 786436
  6.5 270.1 %reduce-scatter.4.cloned.1.call-start = ((), (), s32[]{:S(2)}) async-start(), calls=%async_computation.2 | async-start | bytes 8912896
  19.6 1.7 slice-start
  35.5 1.7 slice-start
  51.4 1.7 slice-start
  67.3 1.7 slice-start
  83.2 1.7 slice-start
  99.1 1.7 slice-start
  115.0 1.7 slice-start
  130.9 1.7 slice-start
  278.3 7.2 copy-start.2
  278.3 7.2 copy-start.3
  725.5 0.7 copy-start.1
Sparse Core Ops, SparseCore 0:
  184.2 92.4 reduce-scatter.3
where the time goes:
time: 739 us; the launch traced here: 733 us
  loops' own time  253 us (34%)
  local copies, waits for them, and re-layouts  221 us (30%)
  other arithmetic  112 us (15%)
  waiting for transfers between devices  92.6 us (13%)
  matrix products  34.5 us (5%)
  between operations  14.2 us (2%)
    another operation x1, loops' own time, coherent(): lax.fori_loop(0, delays.shape[0], direction, jnp.zeros((height, window),...  253 us
    max x64, other arithmetic, direction(): return jnp.maximum(highest, jnp.abs(summed))  101 us
    unnamed x2, waiting for transfers between devices  92.6 us
    reshape x8, local copies, waits for them, and re-layouts, hankel_block(): tiled.reshape(block_rows, length - 1)  44.2 us
    dynamic_slice x64, local copies, waits for them, and re-layouts, direction(): summed = summed + antenna[number, detector] * shifted  42.1 us
    dynamic_slice x64, local copies, waits for them, and re-layouts, direction(): delays[number, detector]  41.9 us
    another operation x16, local copies, waits for them, and re-layouts, hankel_block(): tiled = jnp.tile(backward, block_rows + 1)[:block_rows * (length - 1)]  38 us
    dot_general x8, matrix products, one_block(): jnp.einsum('bt,it->bi', taps_bank, toeplitz, preferred_element_type=jnp.f...  28.3 us
  transfers between devices with their start and end apart: 1, of which 1 were waited for; matrix products, arithmetic and copies ran while one was open for 0% of the time, Pallas kernels for 0%

commit v1 on v0

v1 whole, which is shorter than its diff:
```python
import jax
import jax.numpy as jnp
from jax import lax
from jax.experimental import pallas as pl
from jax.experimental.pallas import tpu as pltpu
from jax.sharding import PartitionSpec as P

PHASES = 16
LANES = 128
BLOCK = 256


def interleave(tiles, lane):
    def swap(tiles, bit, lane_bit):
        step = 1 << lane_bit
        upper = (lane & step) != 0
        result = list(tiles)
        for v in range(PHASES):
            if v & (1 << bit):
                continue
            low, high = tiles[v], tiles[v | (1 << bit)]
            result[v] = jnp.where(upper, pltpu.roll(high, step, 1), low)
            result[v | (1 << bit)] = jnp.where(upper, high, pltpu.roll(low, LANES - step, 1))
        return result

    for bit in range(4):
        tiles = swap(tiles, bit, bit)
    for bit in range(3):
        tiles = swap(tiles, bit, bit + 4)
    return tiles


def kernel(rates, delays, antenna, g_ref, v_ref, out_ref, toeplitz, hankel, full, half, small, spread):
    step = pl.program_id(0)
    last = pl.num_programs(0) - 1
    rows, taps = g_ref.shape[1], g_ref.shape[2]
    detectors, blocks = v_ref.shape[1], v_ref.shape[2]
    depth = taps // BLOCK + 1
    directions = delays.shape[0]

    @pl.when(step == 0)
    def _():
        full[...] = jnp.zeros_like(full)
        half[...] = jnp.zeros_like(half)
        small[...] = jnp.zeros_like(small)

    lane8 = lax.broadcasted_iota(jnp.int32, (8, LANES), 1)
    turn = 16 + 16 * lax.broadcasted_iota(jnp.int32, (8, LANES), 0)
    first = lane8 < turn

    def turned(k, a, tile):
        piece = v_ref[0, k, a : a + 1, tile * LANES : (tile + 1) * LANES]
        return pltpu.roll(jnp.broadcast_to(piece, (8, LANES)), 16, 1, stride=16, stride_axis=0)

    for k in range(detectors):
        behind = jnp.zeros((8, LANES), jnp.float32)
        older = jnp.zeros((8, LANES), jnp.float32)
        for a in range(blocks):
            now0, now1 = turned(k, a, 0), turned(k, a, 1)
            near = jnp.where(first, now0, now1)
            far = jnp.where(first, now1, behind)
            hankel[k, a, :, 0:LANES] = jnp.concatenate([far, near], axis=0).astype(jnp.bfloat16)
            hankel[k, a, :, LANES:] = jnp.concatenate([older, far], axis=0).astype(jnp.bfloat16)
            behind, older = now0, near

    padded = jnp.concatenate([g_ref[0], jnp.zeros((rows, BLOCK), jnp.float32)], axis=1)
    for p in range(PHASES):
        shift = PHASES - 1 - p
        moved = padded if shift == 0 else pltpu.roll(padded, shift, 1)
        toeplitz[p * rows : (p + 1) * rows, :] = moved.astype(jnp.bfloat16)

    def convolve(groups):
        sides = []
        for k in range(detectors):
            sides.append(
                jnp.concatenate(
                    [
                        hankel[k, depth - 1 - c : depth - 1 - c + groups].reshape(groups * 16, BLOCK)
                        for c in range(depth)
                    ],
                    axis=1,
                )
            )
        return lax.dot_general(
            toeplitz[...],
            jnp.concatenate(sides, axis=0),
            (((1,), (1,)), ((), ())),
            preferred_element_type=jnp.float32,
        )

    rate = rates[step]

    @pl.when(rate == 1)
    def _():
        full[...] += convolve(16)

    @pl.when(rate == 2)
    def _():
        half[...] += convolve(8)

    @pl.when(rate > 2)
    def _():
        small[(rate > 4).astype(jnp.int32)] += convolve(4)

    @pl.when(step == last)
    def _():
        lane = lax.broadcasted_iota(jnp.int32, (rows, LANES), 1)
        for k in range(detectors):
            for tile in range(2):
                q = lane + tile * LANES
                total = [
                    full[p * rows : (p + 1) * rows, (2 * k + tile) * LANES : (2 * k + tile + 1) * LANES]
                    for p in range(PHASES)
                ]
                for level in (1, 2, 3):
                    each, count = 1 << level, PHASES >> level
                    source = (q >> level) + (0 if level == 1 else 64 * k)
                    for c in range(count):
                        value = None
                        for phase in range(each):
                            p = phase * count + c
                            if level == 1:
                                piece = half[p * rows : (p + 1) * rows, k * LANES : (k + 1) * LANES]
                            else:
                                piece = small[level - 2, p * rows : (p + 1) * rows, :]
                            piece = jnp.take_along_axis(piece, source, axis=1)
                            value = piece if value is None else jnp.where((q & (each - 1)) == phase, piece, value)
                        for p in range(c * each, (c + 1) * each):
                            total[p] = total[p] + value
                for p in range(PHASES):
                    spread[k, p, :, tile * LANES : (tile + 1) * LANES] = total[p]
            ending = lane == LANES - 1
            for a in range(1, 4):
                for p in range(PHASES):
                    low = pltpu.roll(spread[k, (a - 1) * PHASES + p, :, 0:LANES], LANES - 1, 1)
                    high = pltpu.roll(spread[k, (a - 1) * PHASES + p, :, LANES:], LANES - 1, 1)
                    spread[k, a * PHASES + p, :, 0:LANES] = jnp.where(ending, high, low)
                    spread[k, a * PHASES + p, :, LANES:] = jnp.where(ending, 0.0, high)
        group = 4
        tiles = [[], []]
        for start in range(0, PHASES, group):

            def direction(number, highest):
                one = antenna[number, 0] * spread[0, pl.ds(start + delays[number, 0], group)]
                two = antenna[number, 1] * spread[1, pl.ds(start + delays[number, 1], group)]
                return jnp.maximum(highest, jnp.abs(one + two))

            highest = lax.fori_loop(
                0, directions, direction, jnp.zeros((group, rows, 2 * LANES), jnp.float32), unroll=2
            )
            for p in range(group):
                full[(start + p) * rows : (start + p + 1) * rows, 0 : 2 * LANES] = highest[p]
        for tile in range(2):
            mixed = interleave(
                [full[p * rows : (p + 1) * rows, tile * LANES : (tile + 1) * LANES] for p in range(PHASES)], lane
            )
            for v in range(PHASES):
                at = 16 * tile + ((v & 7) << 1) + (v >> 3)
                out_ref[:, at * LANES : (at + 1) * LANES] = mixed[v]


def shards(strain, filters, recon_weights, row_spans, slice_rates, delays, antenna):
    slice_index = lax.axis_index("cuts")
    slices = lax.axis_size("cuts")
    detector = lax.axis_index("det")
    detectors = lax.axis_size("det")
    bases, taps = filters.shape[1:]
    share = recon_weights.shape[1] // (slices * detectors)
    window = strain.shape[2] - taps
    blocks = strain.shape[2] // BLOCK
    weights = lax.dynamic_index_in_dim(
        recon_weights[0].reshape(slices, detectors, share, bases), detector, 1, keepdims=False
    )
    spans = lax.dynamic_index_in_dim(row_spans.reshape(slices, detectors, share), detector, 1, keepdims=False)
    composite = jnp.dot(weights.reshape(slices * share, bases), filters[0], preferred_element_type=jnp.float32)
    composite = composite.reshape(slices, share, taps) * (slice_index < spans).astype(jnp.float32)[:, :, None]
    exchange = (lax.broadcasted_iota(jnp.int32, (BLOCK, BLOCK), 0) + lax.broadcasted_iota(jnp.int32, (BLOCK, BLOCK), 1)
                == BLOCK - 1).astype(jnp.bfloat16)
    backward = jnp.dot(strain[0, 0].reshape(blocks, BLOCK), exchange, preferred_element_type=jnp.float32)
    backward = lax.all_gather(backward, ("cuts", "det")).reshape(slices, detectors, blocks, BLOCK)
    received = lax.all_to_all(composite, "cuts", split_axis=0, concat_axis=0, tiled=True)
    depth = taps + BLOCK
    return pl.pallas_call(
        kernel,
        out_shape=jax.ShapeDtypeStruct((share, window), jnp.float32),
        grid_spec=pltpu.PrefetchScalarGridSpec(
            num_scalar_prefetch=3,
            grid=(slices,),
            in_specs=[
                pl.BlockSpec((1, share, taps), lambda i, *_: (i, 0, 0)),
                pl.BlockSpec((1, detectors, blocks, BLOCK), lambda i, *_: (i, 0, 0, 0)),
            ],
            out_specs=pl.BlockSpec((share, window), lambda i, *_: (0, 0)),
            scratch_shapes=[
                pltpu.VMEM((PHASES * share, depth), jnp.bfloat16),
                pltpu.VMEM((detectors, blocks, 16, BLOCK), jnp.bfloat16),
                pltpu.VMEM((PHASES * share, detectors * 256), jnp.float32),
                pltpu.VMEM((PHASES * share, detectors * 128), jnp.float32),
                pltpu.VMEM((2, PHASES * share, detectors * 64), jnp.float32),
                pltpu.VMEM((detectors, 4 * PHASES, share, 256), jnp.float32),
            ],
        ),
        compiler_params=pltpu.CompilerParams(
            vmem_limit_bytes=32 * 1024 * 1024, dimension_semantics=("arbitrary",)
        ),
    )(slice_rates, delays, antenna, received, backward)


def solution(mesh):
    placed = (
        P("cuts", "det", None),
        P(("bank", "cuts"), None, None),
        P(("bank", "cuts"), None, None),
        P("bank"),
        P(),
        P(),
        P(),
    )
    return jax.shard_map(
        shards,
        mesh=mesh,
        in_specs=placed,
        out_specs=P(("bank", "cuts", "det"), None),
        check_vma=False,
    )
```

time: 739 us -> 84.8 us (0.11)
  loops' own time: 253 us -> 0 us
  local copies, waits for them, and re-layouts: 221 us -> 2.56 us
  other arithmetic: 112 us -> 0.09 us
  waiting for transfers between devices: 92.6 us -> 0.01 us
  blocking collectives: 5.93 us -> 47.6 us
  matrix products: 34.5 us -> 2.84 us
  Pallas kernels: 0 us -> 23.5 us
  between operations: 14.2 us -> 0.06 us
  starting transfers between devices: 0.01 us -> 7.73 us
    another operation x2 -> x0, loops' own time: 253 us -> none  [the longest x1 253 us: coherent(): lax.fori_loop(0, delays.shape[0], direction, jnp.zeros((height, window),...]
    max x64 -> x0, other arithmetic: 101 us -> none  [direction(): return jnp.maximum(highest, jnp.abs(summed))]
    unnamed x2 -> x0, waiting for transfers between devices: 92.6 us -> none
    dynamic_slice x137 -> x0, local copies, waits for them, and re-layouts: 86 us -> none  [the longest x64 42.1 us: direction(): summed = summed + antenna[number, detector] * shifted]
    all_gather x0 -> x1, blocking collectives: none -> 47.6 us  [shards(): lax.all_gather(backward, ('cuts', 'det'))]
    reshape x9 -> x1, local copies, waits for them, and re-layouts: 45.1 us -> 0.86 us  [shards(): row_spans.reshape(slices, detectors, share)]
    another operation x16 -> x1, local copies, waits for them, and re-layouts: 38 us -> 0.01 us  [shards(): strain[0, 0].reshape(blocks, BLOCK)]
    dot_general x9 -> x2, matrix products: 34.5 us -> 2.84 us  [the longest x1 2.69 us: shards(): jnp.dot(weights.reshape(slices * share, bases), filters[0], preferred_ele...]
  transfers between devices with their start and end apart: 1 -> 1, of which waited for: 1 -> 0; matrix products, arithmetic and copies ran while one was open for 0% -> 1% of each run, Pallas kernels for 0% -> 0%
where the time goes in v1:
time: 84.8 us; the launch traced here: 84.3 us
  blocking collectives  47.6 us (56%)
  Pallas kernels  23.5 us (28%)
  starting transfers between devices  7.73 us (9%)
  matrix products  2.84 us (3%)
  local copies, waits for them, and re-layouts  2.56 us (3%)
    all_gather x1, blocking collectives, shards(): lax.all_gather(backward, ('cuts', 'det'))  47.6 us
    pallas_call x1, Pallas kernels, shards(): pl.pallas_call(kernel, out_shape=jax.ShapeDtypeStruct((share, window), jn...  23.5 us
    all_to_all x1, starting transfers between devices, shards(): lax.all_to_all(composite, 'cuts', split_axis=0, concat_axis=0, tiled=True)  7.73 us
    dot_general x1, matrix products, shards(): jnp.dot(weights.reshape(slices * share, bases), filters[0], preferred_ele...  2.69 us
  transfers between devices with their start and end apart: 1, of which 0 were waited for; matrix products, arithmetic and copies ran while one was open for 1% of the time, Pallas kernels for 0%

profile of v1, /device:TPU:1, one launch (start us, length us, event | category | flops | bytes accessed | tf_op | source)
XLA Modules:
  0.0 84.3 jit_solution(8097850772959876194)
XLA Ops:
  0.0 0.0 copy-start
  0.0 0.9 %reshape.21 = s32[16,2,16]{2,1,0:T(2,128)S(1)} reshape(s32[512]{0:T(512)} %param.10) | data formatting | bytes 4096 | tf_op jit(solution)/shard_map/reshape | solution.py:174
  0.9 0.3 copy-done
  1.2 2.7 %convolution_multiply_fusion = f32[16,16,2048]{2,1,0:T(8,128)} fusion(bf16[1,256,2048]{2,1,0:T(8,128)(2,1)S(1)} %copy-done, f32[16,16]{1,0:T(8,128)S(1)} %bitcast.17, bf16[16,2,16,256]{3,2,1,0:T(8,128)(2,1)} %bitcast.16, s32[]{:T(128)S(6)} %select_n.6), kind=kOutput, calls=%fused_computation | convolution fusion | flops 268959744 | bytes 3277828 | tf_op jit(solution)/shard_map/dot_general | solution.py:175
  3.9 0.0 copy-start.3
  3.9 0.0 copy-start.4
  3.9 0.0 copy-start.5
  3.9 0.0 copy-start.2
  3.9 7.7 %all-to-all-start = ((f32[16,16,2048]{2,1,0:T(8,128)}), f32[16,16,2048]{2,1,0:T(8,128)S(1)}, u32[]{:S(2)}, u32[]{:S(2)}) async-start(f32[16,16,2048]{2,1,0:T(8,128)} %convolution_multiply_fusion), calls=%async_computation | async-start | bytes 4194304 | tf_op jit(solution)/shard_map/all_to_all | solution.py:181
  11.7 0.0 copy-done.3
  11.7 0.1 reduce
  11.8 0.0 copy-done.4
  11.8 0.1 copy.12.delays
  11.9 0.0 copy-done.5
  11.9 0.1 copy.13.antenna
  12.0 0.2 convolution_bitcast_fusion
  12.1 47.6 %all-gather = f32[768,256]{1,0:T(8,128)} all-gather(f32[24,256]{1,0:T(8,128)S(1)} %convolution_bitcast_fusion), channel_id=2, replica_groups=mesh['cuts'=16,'det'=2,'bank'=8] {'cuts','det'}, dimensions={0}, use_global_device_ids=true | all-gather | bytes 811008 | tf_op jit(solution)/shard_map/all_gather | solution.py:180
  59.7 0.0 all-to-all-done.g_ref
  59.7 0.0 copy-done.2
  59.7 0.0 copy-start.1
  59.7 1.1 %copy-done.1 = f32[768,256]{1,0:T(8,128)S(1)} copy-done((f32[768,256]{1,0:T(8,128)S(1)}, f32[768,256]{1,0:T(8,128)}, u32[]{:S(2)}) %copy-start.1) | copy-done | bytes 786456
  60.8 23.5 %shard_map.73 = f32[16,4096]{1,0:T(8,128)} custom-call(s32[16]{0:T(128)S(1)} %copy-done.2, s32[64,2]{1,0:T(8,128)S(1)} %copy.12.delays, f32[64,2]{1,0:T(8,128)S(1)} %copy.13.antenna, f32[16,16,2048]{2,1,0:T(8,128)S(1)} %all-to-all-done.g_ref, f32[16,2,24,256]{3,2,1,0:T(8,128)S(1)} %bitcast.15), custom_call_target="tpu_custom_call" | custom-call | tf_op jit(solution)/shard_map/pallas_call | solution.py:183
  (2 shorter events, 0.0 us)
Async XLA Ops:
  0.0 1.2 %copy-start = (bf16[1,256,2048]{2,1,0:T(8,128)(2,1)S(1)}, bf16[1,256,2048]{2,1,0:T(8,128)(2,1)}, u32[]{:S(2)}) copy-start(bf16[1,256,2048]{2,1,0:T(8,128)(2,1)} %param.8) | copy-start | bytes 3145732
  3.9 7.7 %copy-start.3 = (bf16[1,1,6144]{2,1,0:T(2,128)(2,1)S(1)}, bf16[1,1,6144]{2,1,0:T(2,128)(2,1)}, u32[]{:S(2)}) copy-start(bf16[1,1,6144]{2,1,0:T(2,128)(2,1)} %param.7) | copy-start | bytes 36868
  3.9 7.8 %copy-start.4 = (s32[64,2]{0,1:T(2,128)S(1)}, s32[64,2]{0,1:T(2,128)}, u32[]{:S(2)}) copy-start(s32[64,2]{0,1:T(2,128)} %param.12) | copy-start | bytes 1540
  3.9 8.0 %copy-start.5 = (f32[64,2]{0,1:T(2,128)S(1)}, f32[64,2]{0,1:T(2,128)}, u32[]{:S(2)}) copy-start(f32[64,2]{0,1:T(2,128)} %param.13) | copy-start | bytes 1540
  3.9 55.8 %copy-start.2 = (s32[16]{0:T(128)S(1)}, s32[16]{0:T(128)}, u32[]{:S(2)}) copy-start(s32[16]{0:T(128)} %rates.1) | copy-start | bytes 196
  3.9 55.8 %all-to-all-start = ((f32[16,16,2048]{2,1,0:T(8,128)}), f32[16,16,2048]{2,1,0:T(8,128)S(1)}, u32[]{:S(2)}, u32[]{:S(2)}) async-start(f32[16,16,2048]{2,1,0:T(8,128)} %convolution_multiply_fusion), calls=%async_computation | async-start | bytes 4194304 | tf_op jit(solution)/shard_map/all_to_all | solution.py:181
  59.7 1.1 %copy-start.1 = (f32[768,256]{1,0:T(8,128)S(1)}, f32[768,256]{1,0:T(8,128)}, u32[]{:S(2)}) copy-start(f32[768,256]{1,0:T(8,128)} %all-gather) | copy-start | bytes 2359300

commit v2 on v1

--- a/solution.py
+++ b/solution.py
@@ -8,6 +8,33 @@
 PHASES = 16
 LANES = 128
 BLOCK = 256
+
+
+def compose(weights_ref, filters_ref, strain_ref, out_ref):
+    step = pl.program_id(0)
+    last = pl.num_programs(0) - 1
+    targets, share = out_ref.shape[0], weights_ref.shape[1]
+    tiles = out_ref.shape[1] // share
+
+    @pl.when(step < last)
+    def _():
+        rows = jnp.dot(
+            weights_ref[...].reshape(targets * share, -1), filters_ref[...], preferred_element_type=jnp.float32
+        )
+        for tile in range(tiles):
+            out_ref[:, tile * share : (tile + 1) * share, :] = rows[:, tile * LANES : (tile + 1) * LANES].reshape(
+                targets, share, LANES
+            )
+
+    @pl.when(step == last)
+    def _():
+        flip = (
+            lax.broadcasted_iota(jnp.int32, (LANES, LANES), 0) + lax.broadcasted_iota(jnp.int32, (LANES, LANES), 1)
+            == LANES - 1
+        ).astype(jnp.bfloat16)
+        backward = jnp.dot(strain_ref[...], flip, preferred_element_type=jnp.float32)
+        for target in range(targets):
+            out_ref[target, 0 : backward.shape[0], :] = backward
 
 
 def interleave(tiles, lane):
@@ -30,11 +57,13 @@
     return tiles
 
 
-def kernel(rates, delays, antenna, g_ref, v_ref, out_ref, toeplitz, hankel, full, half, small, spread):
+def kernel(rates, spans, delays, antenna, place, g_ref, other_ref, out_ref, toeplitz, hankel, full, half, small, spread, keep):
     step = pl.program_id(0)
     last = pl.num_programs(0) - 1
-    rows, taps = g_ref.shape[1], g_ref.shape[2]
-    detectors, blocks = v_ref.shape[1], v_ref.shape[2]
+    rows = out_ref.shape[0]
+    tiles = (g_ref.shape[1] - other_ref.shape[1]) // rows
+    taps = tiles * LANES
+    detectors, blocks = hankel.shape[0], hankel.shape[1]
     depth = taps // BLOCK + 1
     directions = delays.shape[0]
 
@@ -43,33 +72,46 @@
         full[...] = jnp.zeros_like(full)
         half[...] = jnp.zeros_like(half)
         small[...] = jnp.zeros_like(small)
+        row = lax.broadcasted_iota(jnp.int32, (rows, LANES), 0)
+        span = jnp.zeros((rows, LANES), jnp.int32)
+        for r in range(rows):
+            span = jnp.where(row == r, spans[place[0] * rows + r], span)
+        keep[...] = span
 
     lane8 = lax.broadcasted_iota(jnp.int32, (8, LANES), 1)
     turn = 16 + 16 * lax.broadcasted_iota(jnp.int32, (8, LANES), 0)
     first = lane8 < turn
 
-    def turned(k, a, tile):
-        piece = v_ref[0, k, a : a + 1, tile * LANES : (tile + 1) * LANES]
-        return pltpu.roll(jnp.broadcast_to(piece, (8, LANES)), 16, 1, stride=16, stride_axis=0)
-
-    for k in range(detectors):
-        behind = jnp.zeros((8, LANES), jnp.float32)
-        older = jnp.zeros((8, LANES), jnp.float32)
-        for a in range(blocks):
-            now0, now1 = turned(k, a, 0), turned(k, a, 1)
-            near = jnp.where(first, now0, now1)
-            far = jnp.where(first, now1, behind)
-            hankel[k, a, :, 0:LANES] = jnp.concatenate([far, near], axis=0).astype(jnp.bfloat16)
-            hankel[k, a, :, LANES:] = jnp.concatenate([older, far], axis=0).astype(jnp.bfloat16)
-            behind, older = now0, near
-
-    padded = jnp.concatenate([g_ref[0], jnp.zeros((rows, BLOCK), jnp.float32)], axis=1)
-    for p in range(PHASES):
-        shift = PHASES - 1 - p
-        moved = padded if shift == 0 else pltpu.roll(padded, shift, 1)
-        toeplitz[p * rows : (p + 1) * rows, :] = moved.astype(jnp.bfloat16)
+    def windows():
+        for k, (ref, base) in enumerate(((g_ref, tiles * rows), (other_ref, 0))):
+
+            def turned(a, tile):
+                at = base + 2 * a + 1 - tile
+                piece = ref[0, at : at + 1, :]
+                return pltpu.roll(jnp.broadcast_to(piece, (8, LANES)), 16, 1, stride=16, stride_axis=0)
+
+            behind = jnp.zeros((8, LANES), jnp.float32)
+            older = jnp.zeros((8, LANES), jnp.float32)
+            for a in range(blocks):
+                now0, now1 = turned(a, 0), turned(a, 1)
+                near = jnp.where(first, now0, now1)
+                far = jnp.where(first, now1, behind)
+                hankel[k, a, :, 0:LANES] = jnp.concatenate([far, near], axis=0).astype(jnp.bfloat16)
+                hankel[k, a, :, LANES:] = jnp.concatenate([older, far], axis=0).astype(jnp.bfloat16)
+                behind, older = now0, near
+
+    def shifted():
+        kept = (step < keep[...]).astype(jnp.float32)
+        parts = [g_ref[0, t * rows : (t + 1) * rows, :] * kept for t in range(tiles)]
+        padded = jnp.concatenate(parts + [jnp.zeros((rows, BLOCK), jnp.float32)], axis=1)
+        for p in range(PHASES):
+            shift = PHASES - 1 - p
+            moved = padded if shift == 0 else pltpu.roll(padded, shift, 1)
+            toeplitz[p * rows : (p + 1) * rows, :] = moved.astype(jnp.bfloat16)
 
     def convolve(groups):
+        windows()
+        shifted()
         sides = []
         for k in range(detectors):
             sides.append(
@@ -136,17 +178,17 @@
                     high = pltpu.roll(spread[k, (a - 1) * PHASES + p, :, LANES:], LANES - 1, 1)
                     spread[k, a * PHASES + p, :, 0:LANES] = jnp.where(ending, high, low)
                     spread[k, a * PHASES + p, :, LANES:] = jnp.where(ending, 0.0, high)
+        own, other = place[1], 1 - place[1]
         group = 4
-        tiles = [[], []]
         for start in range(0, PHASES, group):
 
             def direction(number, highest):
-                one = antenna[number, 0] * spread[0, pl.ds(start + delays[number, 0], group)]
-                two = antenna[number, 1] * spread[1, pl.ds(start + delays[number, 1], group)]
+                one = antenna[number, own] * spread[0, pl.ds(start + delays[number, own], group)]
+                two = antenna[number, other] * spread[1, pl.ds(start + delays[number, other], group)]
                 return jnp.maximum(highest, jnp.abs(one + two))
 
             highest = lax.fori_loop(
-                0, directions, direction, jnp.zeros((group, rows, 2 * LANES), jnp.float32), unroll=2
+                0, directions, direction, jnp.zeros((group, rows, 2 * LANES), jnp.float32), unroll=8
             )
             for p in range(group):
                 full[(start + p) * rows : (start + p + 1) * rows, 0 : 2 * LANES] = highest[p]
@@ -167,43 +209,56 @@
     bases, taps = filters.shape[1:]
     share = recon_weights.shape[1] // (slices * detectors)
     window = strain.shape[2] - taps
-    blocks = strain.shape[2] // BLOCK
-    weights = lax.dynamic_index_in_dim(
-        recon_weights[0].reshape(slices, detectors, share, bases), detector, 1, keepdims=False
-    )
-    spans = lax.dynamic_index_in_dim(row_spans.reshape(slices, detectors, share), detector, 1, keepdims=False)
-    composite = jnp.dot(weights.reshape(slices * share, bases), filters[0], preferred_element_type=jnp.float32)
-    composite = composite.reshape(slices, share, taps) * (slice_index < spans).astype(jnp.float32)[:, :, None]
-    exchange = (lax.broadcasted_iota(jnp.int32, (BLOCK, BLOCK), 0) + lax.broadcasted_iota(jnp.int32, (BLOCK, BLOCK), 1)
-                == BLOCK - 1).astype(jnp.bfloat16)
-    backward = jnp.dot(strain[0, 0].reshape(blocks, BLOCK), exchange, preferred_element_type=jnp.float32)
-    backward = lax.all_gather(backward, ("cuts", "det")).reshape(slices, detectors, blocks, BLOCK)
-    received = lax.all_to_all(composite, "cuts", split_axis=0, concat_axis=0, tiled=True)
+    tiles = strain.shape[2] // LANES
+    place = jnp.stack([slice_index * detectors + detector, detector]).astype(jnp.int32)
+    steps = 4
+    body = taps // steps // LANES * share
+    message = pl.pallas_call(
+        lambda place, *refs: compose(*refs),
+        out_shape=jax.ShapeDtypeStruct((slices, taps // LANES * share + tiles, LANES), jnp.float32),
+        grid_spec=pltpu.PrefetchScalarGridSpec(
+            num_scalar_prefetch=1,
+            grid=(steps + 1,),
+            in_specs=[
+                pl.BlockSpec((slices, None, share, bases), lambda i, place: (0, place[1], 0, 0)),
+                pl.BlockSpec((None, bases, taps // steps), lambda i, place: (0, 0, jnp.minimum(i, steps - 1))),
+                pl.BlockSpec((tiles, LANES), lambda i, place: (0, 0)),
+            ],
+            out_specs=pl.BlockSpec((slices, body, LANES), lambda i, place: (0, i, 0)),
+        ),
+        compiler_params=pltpu.CompilerParams(
+            vmem_limit_bytes=32 * 1024 * 1024, dimension_semantics=("arbitrary",)
+        ),
+    )(place, recon_weights.reshape(slices, detectors, share, bases), filters, strain.reshape(tiles, LANES))
+    received = lax.all_to_all(message, "cuts", split_axis=0, concat_axis=0, tiled=True)
+    body = taps // LANES * share
+    partner = lax.ppermute(received[:, body:], "det", [(0, 1), (1, 0)])
     depth = taps + BLOCK
     return pl.pallas_call(
         kernel,
         out_shape=jax.ShapeDtypeStruct((share, window), jnp.float32),
         grid_spec=pltpu.PrefetchScalarGridSpec(
-            num_scalar_prefetch=3,
+            num_scalar_prefetch=5,
             grid=(slices,),
             in_specs=[
-                pl.BlockSpec((1, share, taps), lambda i, *_: (i, 0, 0)),
-                pl.BlockSpec((1, detectors, blocks, BLOCK), lambda i, *_: (i, 0, 0, 0)),
+                pl.BlockSpec((1, body + tiles, LANES), lambda i, *_: (i, 0, 0)),
+                pl.BlockSpec((1, tiles, LANES), lambda i, *_: (i, 0, 0)),
             ],
             out_specs=pl.BlockSpec((share, window), lambda i, *_: (0, 0)),
             scratch_shapes=[
                 pltpu.VMEM((PHASES * share, depth), jnp.bfloat16),
-                pltpu.VMEM((detectors, blocks, 16, BLOCK), jnp.bfloat16),
+                pltpu.VMEM((detectors, tiles // 2, 16, BLOCK), jnp.bfloat16),
                 pltpu.VMEM((PHASES * share, detectors * 256), jnp.float32),
                 pltpu.VMEM((PHASES * share, detectors * 128), jnp.float32),
                 pltpu.VMEM((2, PHASES * share, detectors * 64), jnp.float32),
                 pltpu.VMEM((detectors, 4 * PHASES, share, 256), jnp.float32),
+                pltpu.VMEM((share, LANES), jnp.int32),
             ],
         ),
         compiler_params=pltpu.CompilerParams(
             vmem_limit_bytes=32 * 1024 * 1024, dimension_semantics=("arbitrary",)
         ),
-    )(slice_rates, delays, antenna, received, backward)
+    )(slice_rates, row_spans, delays, antenna, place, received, partner)
 
 
 def solution(mesh):

time: 84.8 us -> 66.6 us (0.79)
  blocking collectives: 47.6 us -> 38.4 us
  starting transfers between devices: 7.73 us -> 2.41 us
  matrix products: 2.84 us -> 0 us
  Pallas kernels: 23.5 us -> 20.7 us
  waiting for transfers between devices: 0.01 us -> 1.15 us
    all_gather x1 -> x0, blocking collectives: 47.6 us -> none  [shards(): lax.all_gather(backward, ('cuts', 'det'))]
    all_to_all x0 -> x1, blocking collectives: none -> 38.4 us  [shards(): lax.all_to_all(message, 'cuts', split_axis=0, concat_axis=0, tiled=True)]
    all_to_all x1 -> x0, starting transfers between devices: 7.73 us -> none  [shards(): lax.all_to_all(composite, 'cuts', split_axis=0, concat_axis=0, tiled=True)]
    pallas_call x1, Pallas kernels: 23.5 us -> 18.6 us  [shards(): pl.pallas_call(kernel, out_shape=jax.ShapeDtypeStruct((share, window), jn...]
    dot_general x2 -> x0, matrix products: 2.84 us -> none  [the longest x1 2.69 us: shards(): jnp.dot(weights.reshape(slices * share, bases), filters[0], preferred_ele...]
    ppermute x0 -> x1, starting transfers between devices: none -> 2.41 us  [shards(): partner = lax.ppermute(received[:, body:], 'det', [(0, 1), (1, 0)])]
    pallas_call x0 -> x1, Pallas kernels: none -> 2.1 us  [shards(): pl.pallas_call(lambda place, *refs: compose(*refs), out_shape=jax.ShapeDt...]
    ppermute x0 -> x1, waiting for transfers between devices: none -> 1.15 us  [shards(): partner = lax.ppermute(received[:, body:], 'det', [(0, 1), (1, 0)])]
  transfers between devices with their start and end apart: 1 -> 1, of which waited for: 0 -> 1; matrix products, arithmetic and copies ran while one was open for 1% -> 0% of each run, Pallas kernels for 0% -> 0%
where the time goes in v2:
time: 66.6 us; the launch traced here: 66 us
  blocking collectives  38.4 us (58%)
  Pallas kernels  20.7 us (31%)
  local copies, waits for them, and re-layouts  2.41 us (4%)
  starting transfers between devices  2.41 us (4%)
  waiting for transfers between devices  1.15 us (2%)
  other arithmetic  0.88 us (1%)
    all_to_all x1, blocking collectives, shards(): lax.all_to_all(message, 'cuts', split_axis=0, concat_axis=0, tiled=True)  38.4 us
    pallas_call x1, Pallas kernels, shards(): pl.pallas_call(kernel, out_shape=jax.ShapeDtypeStruct((share, window), jn...  18.6 us
    ppermute x1, starting transfers between devices, shards(): partner = lax.ppermute(received[:, body:], 'det', [(0, 1), (1, 0)])  2.41 us
    unnamed x14, local copies, waits for them, and re-layouts  2.39 us
    pallas_call x1, Pallas kernels, shards(): pl.pallas_call(lambda place, *refs: compose(*refs), out_shape=jax.ShapeDt...  2.1 us
  transfers between devices with their start and end apart: 1, of which 1 were waited for; matrix products, arithmetic and copies ran while one was open for 0% of the time, Pallas kernels for 0%

profile of v2, /device:TPU:1, one launch (start us, length us, event | category | flops | bytes accessed | tf_op | source)
XLA Modules:
  0.0 66.0 jit_solution(14784017057926937431)
XLA Ops:
  0.0 0.1 pad_add_fusion.place
  0.1 0.8 %reduce = bf16[6144]{0:T(1024)(128)(2,1)S(1)} reduce(bf16[1,1,6144]{2,1,0:T(2,128)(2,1)} %param.7, bf16[]{:T(256)} %constant.16), dimensions={0,1}, to_apply=%param.7.reduce_sub_computation | reduce | bytes 24578 | tf_op args[0]
  0.9 0.0 copy-start
  0.9 1.2 %copy-done = bf16[1,256,2048]{2,1,0:T(8,128)(2,1)S(1)} copy-done((bf16[1,256,2048]{2,1,0:T(8,128)(2,1)S(1)}, bf16[1,256,2048]{2,1,0:T(8,128)(2,1)}, u32[]{:S(2)}) %copy-start) | copy-done | bytes 1048600
  2.1 0.0 copy-start.1
  2.1 0.9 %copy-done.1 = bf16[1,512,256]{2,1,0:T(8,128)(2,1)S(1)} copy-done((bf16[1,512,256]{2,1,0:T(8,128)(2,1)S(1)}, bf16[1,512,256]{2,1,0:T(8,128)(2,1)}, u32[]{:S(2)}) %copy-start.1) | copy-done | bytes 262168
  3.1 2.1 %shard_map.73 = f32[16,304,128]{2,1,0:T(8,128)S(1)} custom-call(s32[2]{0:T(128)S(1)} %pad_add_fusion.place, bf16[16,2,16,256]{3,2,1,0:T(8,128)(2,1)S(1)} %bitcast.4, bf16[1,256,2048]{2,1,0:T(8,128)(2,1)S(1)} %copy-done, bf16[48,128]{1,0:T(8,128)(2,1)S(1)} %bitcast.5), custom_call_target="tpu_custom_call" | custom-call | tf_op jit(solution)/shard_map/pallas_call | solution.py:216
  5.2 0.0 copy-start.4
  5.2 0.0 copy-start.5
  5.2 0.0 copy-start.2
  5.2 0.0 copy-start.3
  5.2 38.4 %all_to_all.5.g_ref = f32[16,304,128]{2,1,0:T(8,128)S(1)} all-to-all(f32[16,304,128]{2,1,0:T(8,128)S(1)} %shard_map.73), channel_id=1, replica_groups=mesh['cuts'=16,'det'=2,'bank'=8] {'cuts'}, dimensions={0} | all-to-all | bytes 4980736 | tf_op jit(solution)/shard_map/all_to_all | solution.py:233
  43.7 2.4 %collective-permute-start = (f32[16,48,128]{2,1,0:T(8,128)S(1)}, f32[16,48,128]{2,1,0:T(8,128)S(1)}, u32[]{:S(2)}, u32[]{:S(2)}) collective-permute-start(f32[16,48,128]{2,1,0:T(8,128)S(1)} %slice.4), channel_id=1, source_target_pairs={{0,8},{8,0},{1,9},{9,1},{2,10},{10,2},{3,11},{11,3},{4,12},{12,4},... | collective-permute-start | bytes 1179656 | tf_op jit(solution)/shard_map/ppermute | solution.py:235
  46.1 0.0 copy-done.4
  46.1 0.1 copy.8.delays
  46.2 0.0 copy-done.5
  46.2 0.1 copy.9.antenna
  46.3 1.2 %collective-permute-done.other_ref = f32[16,48,128]{2,1,0:T(8,128)S(1)} collective-permute-done((f32[16,48,128]{2,1,0:T(8,128)S(1)}, f32[16,48,128]{2,1,0:T(8,128)S(1)}, u32[]{:S(2)}, u32[]{:S(2)}) %collective-permute-start) | collective-permute-done | bytes 393248 | tf_op jit(solution)/shard_map/ppermute | solution.py:235
  47.5 0.0 copy-done.2
  47.5 0.0 copy-done.3
  47.5 18.6 %shard_map.74 = f32[16,4096]{1,0:T(8,128)} custom-call(s32[16]{0:T(128)S(1)} %copy-done.3, s32[512]{0:T(512)S(1)} %copy-done.2, s32[64,2]{1,0:T(8,128)S(1)} %copy.8.delays, f32[64,2]{1,0:T(8,128)S(1)} %copy.9.antenna, s32[2]{0:T(128)S(1)} %pad_add_fusion.place, f32[16,304,128]{2,1,0:T(8,128)S(1)} %all_to_all.5.g_ref, ...), custom_call_target="tpu_custom_call" | custom-call | tf_op jit(solution)/shard_map/pallas_call | solution.py:237
  (1 shorter events, 0.0 us)
Async XLA Ops:
  0.9 1.2 %copy-start = (bf16[1,256,2048]{2,1,0:T(8,128)(2,1)S(1)}, bf16[1,256,2048]{2,1,0:T(8,128)(2,1)}, u32[]{:S(2)}) copy-start(bf16[1,256,2048]{2,1,0:T(8,128)(2,1)} %refs_1_.1) | copy-start | bytes 3145732
  2.1 0.9 %copy-start.1 = (bf16[1,512,256]{2,1,0:T(8,128)(2,1)S(1)}, bf16[1,512,256]{2,1,0:T(8,128)(2,1)}, u32[]{:S(2)}) copy-start(bf16[1,512,256]{2,1,0:T(8,128)(2,1)} %param.9) | copy-start | bytes 786436
  5.2 40.9 %copy-start.4 = (s32[64,2]{0,1:T(2,128)S(1)}, s32[64,2]{0,1:T(2,128)}, u32[]{:S(2)}) copy-start(s32[64,2]{0,1:T(2,128)} %param.12) | copy-start | bytes 1540
  5.2 41.0 %copy-start.5 = (f32[64,2]{0,1:T(2,128)S(1)}, f32[64,2]{0,1:T(2,128)}, u32[]{:S(2)}) copy-start(f32[64,2]{0,1:T(2,128)} %param.13) | copy-start | bytes 1540
  5.2 42.3 %copy-start.2 = (s32[512]{0:T(512)S(1)}, s32[512]{0:T(512)}, u32[]{:S(2)}) copy-start(s32[512]{0:T(512)} %spans.1) | copy-start | bytes 6148
  5.2 42.3 %copy-start.3 = (s32[16]{0:T(128)S(1)}, s32[16]{0:T(128)}, u32[]{:S(2)}) copy-start(s32[16]{0:T(128)} %rates.1) | copy-start | bytes 196
  43.7 3.8 %collective-permute-start = (f32[16,48,128]{2,1,0:T(8,128)S(1)}, f32[16,48,128]{2,1,0:T(8,128)S(1)}, u32[]{:S(2)}, u32[]{:S(2)}) collective-permute-start(f32[16,48,128]{2,1,0:T(8,128)S(1)} %slice.4), channel_id=1, source_target_pairs={{0,8},{8,0},{1,9},{9,1},{2,10},{10,2},{3,11},{11,3},{4,12},{12,4},... | collective-permute-start | bytes 1179656 | tf_op jit(solution)/shard_map/ppermute | solution.py:235

commit v3 on v0

v3 whole, which is shorter than its diff:
```python
import jax
import jax.numpy as jnp
from jax import lax
from jax.experimental import pallas as pl
from jax.experimental.pallas import tpu as pltpu
from jax.sharding import PartitionSpec as P

PHASES = 16
LANES = 128
BLOCK = 256
SLOTS = 4


def compose(place, weights_ref, filters_ref, strain_ref, out_ref, weights, filters, got, arrived):
    chunks, _, width = filters.shape
    targets, share, bases = weights.shape
    here = pltpu.make_async_copy(weights_ref.at[:, place[1]], weights, got)
    here.start()
    parts = [
        pltpu.make_async_copy(
            filters_ref.at[0, :, chunk * width : (chunk + 1) * width], filters.at[chunk], arrived.at[chunk]
        )
        for chunk in range(chunks)
    ]
    for part in parts:
        part.start()
    end = out_ref.shape[1]
    count = strain_ref.shape[0]
    flip = (
        lax.broadcasted_iota(jnp.int32, (LANES, LANES), 0) + lax.broadcasted_iota(jnp.int32, (LANES, LANES), 1)
        == LANES - 1
    ).astype(jnp.bfloat16)
    backward = jnp.dot(strain_ref[...], flip, preferred_element_type=jnp.float32)
    for target in range(targets):
        out_ref[target, end - count : end, :] = backward
    here.wait()
    for chunk, part in enumerate(parts):
        part.wait()
        rows = jnp.dot(
            weights[...].reshape(targets * share, bases), filters[chunk], preferred_element_type=jnp.float32
        )
        for tile in range(width // LANES):
            at = chunk * width // LANES + tile
            out_ref[:, at * share : (at + 1) * share, :] = rows[:, tile * LANES : (tile + 1) * LANES].reshape(
                targets, share, LANES
            )


def interleave(tiles, lane):
    def swap(tiles, bit, lane_bit):
        step = 1 << lane_bit
        upper = (lane & step) != 0
        result = list(tiles)
        for v in range(PHASES):
            if v & (1 << bit):
                continue
            low, high = tiles[v], tiles[v | (1 << bit)]
            result[v] = jnp.where(upper, pltpu.roll(high, step, 1), low)
            result[v | (1 << bit)] = jnp.where(upper, high, pltpu.roll(low, LANES - step, 1))
        return result

    for bit in range(4):
        tiles = swap(tiles, bit, bit)
    for bit in range(3):
        tiles = swap(tiles, bit, bit + 4)
    return tiles


def kernel(rates, spans, delays, antenna, place, g_ref, other_ref, out_ref, toeplitz, hankel, full, half, small, spread):
    slices = g_ref.shape[0]
    detectors, blocks = hankel.shape[1], hankel.shape[2]
    rows = out_ref.shape[0]
    tiles = (g_ref.shape[1] - other_ref.shape[1]) // rows
    taps = tiles * LANES
    depth = taps // BLOCK + 1
    directions = delays.shape[0]

    full[...] = jnp.zeros_like(full)
    half[...] = jnp.zeros_like(half)
    small[...] = jnp.zeros_like(small)
    row = lax.broadcasted_iota(jnp.int32, (rows, LANES), 0)
    keep = jnp.zeros((rows, LANES), jnp.int32)
    for r in range(rows):
        keep = jnp.where(row == r, spans[place[0] * rows + r], keep)
    lane8 = lax.broadcasted_iota(jnp.int32, (8, LANES), 1)
    turn = 16 + 16 * lax.broadcasted_iota(jnp.int32, (8, LANES), 0)
    first = lane8 < turn

    def windows(number, slot, groups):
        for k, (ref, base) in enumerate(((g_ref, tiles * rows), (other_ref, 0))):

            def turned(a, tile):
                at = base + 2 * a + 1 - tile
                piece = ref[number, at : at + 1, :]
                return pltpu.roll(jnp.broadcast_to(piece, (8, LANES)), 16, 1, stride=16, stride_axis=0)

            behind = jnp.zeros((8, LANES), jnp.float32)
            older = jnp.zeros((8, LANES), jnp.float32)
            for a in range(depth - 1 + groups):
                now0, now1 = turned(a, 0), turned(a, 1)
                near = jnp.where(first, now0, now1)
                far = jnp.where(first, now1, behind)
                hankel[slot, k, a, :, 0:LANES] = jnp.concatenate([far, near], axis=0).astype(jnp.bfloat16)
                hankel[slot, k, a, :, LANES:] = jnp.concatenate([older, far], axis=0).astype(jnp.bfloat16)
                behind, older = now0, near

    def shifted(number, slot):
        kept = (number < keep).astype(jnp.float32)
        parts = [g_ref[number, t * rows : (t + 1) * rows, :] * kept for t in range(tiles)]
        padded = jnp.concatenate(parts + [jnp.zeros((rows, BLOCK), jnp.float32)], axis=1).astype(jnp.bfloat16)
        for p in range(PHASES):
            shift = PHASES - 1 - p
            moved = padded if shift == 0 else pltpu.roll(padded, shift, 1)
            toeplitz[p * rows : (p + 1) * rows, slot * depth * BLOCK : (slot + 1) * depth * BLOCK] = moved

    def convolve(number, slots, groups):
        for slot in slots:
            shifted(number + slot, slot)
            windows(number + slot, slot, groups)
        sides = []
        for k in range(detectors):
            sides.append(
                jnp.concatenate(
                    [
                        hankel[slot, k, depth - 1 - c : depth - 1 - c + groups].reshape(groups * 16, BLOCK)
                        for slot in slots
                        for c in range(depth)
                    ],
                    axis=1,
                )
            )
        return lax.dot_general(
            toeplitz[:, slots[0] * depth * BLOCK : (slots[-1] + 1) * depth * BLOCK],
            jnp.concatenate(sides, axis=0),
            (((1,), (1,)), ((), ())),
            preferred_element_type=jnp.float32,
        )

    start = 0
    for total, groups, rate in ((full, 16, 1), (half, 8, 2), (small.at[0], 4, 4), (small.at[1], 4, 8)):
        count = lax.fori_loop(0, slices, lambda i, n, rate=rate: n + (rates[i] == rate).astype(jnp.int32), 0)
        done = start
        size = SLOTS
        while size:
            left = start + count - done

            def several(index, carry, done=done, size=size, total=total, groups=groups):
                total[...] += convolve(done + index * size, tuple(range(size)), groups)
                return carry

            times = left // size
            lax.fori_loop(0, times, several, 0)
            done = done + times * size
            size //= 2
        start = start + count

    lane = lax.broadcasted_iota(jnp.int32, (rows, LANES), 1)
    for k in range(detectors):
        for tile in range(2):
            q = lane + tile * LANES
            total = [
                full[p * rows : (p + 1) * rows, (2 * k + tile) * LANES : (2 * k + tile + 1) * LANES]
                for p in range(PHASES)
            ]
            for level in (1, 2, 3):
                each, count = 1 << level, PHASES >> level
                source = (q >> level) + (0 if level == 1 else 64 * k)
                for c in range(count):
                    value = None
                    for phase in range(each):
                        p = phase * count + c
                        if level == 1:
                            piece = half[p * rows : (p + 1) * rows, k * LANES : (k + 1) * LANES]
                        else:
                            piece = small[level - 2, p * rows : (p + 1) * rows, :]
                        piece = jnp.take_along_axis(piece, source, axis=1)
                        value = piece if value is None else jnp.where((q & (each - 1)) == phase, piece, value)
                    for p in range(c * each, (c + 1) * each):
                        total[p] = total[p] + value
            for p in range(PHASES):
                spread[k, p, :, tile * LANES : (tile + 1) * LANES] = total[p]
        ending = lane == LANES - 1
        for a in range(1, 4):
            for p in range(PHASES):
                low = pltpu.roll(spread[k, (a - 1) * PHASES + p, :, 0:LANES], LANES - 1, 1)
                high = pltpu.roll(spread[k, (a - 1) * PHASES + p, :, LANES:], LANES - 1, 1)
                spread[k, a * PHASES + p, :, 0:LANES] = jnp.where(ending, high, low)
                spread[k, a * PHASES + p, :, LANES:] = jnp.where(ending, 0.0, high)
    own, other = place[1], 1 - place[1]
    group = 4
    for start in range(0, PHASES, group):

        def direction(number, highest):
            one = antenna[number, own] * spread[0, pl.ds(start + delays[number, own], group)]
            two = antenna[number, other] * spread[1, pl.ds(start + delays[number, other], group)]
            return jnp.maximum(highest, jnp.abs(one + two))

        highest = lax.fori_loop(
            0, directions, direction, jnp.zeros((group, rows, 2 * LANES), jnp.float32), unroll=8
        )
        for p in range(group):
            full[(start + p) * rows : (start + p + 1) * rows, 0 : 2 * LANES] = highest[p]
    for tile in range(2):
        mixed = interleave(
            [full[p * rows : (p + 1) * rows, tile * LANES : (tile + 1) * LANES] for p in range(PHASES)], lane
        )
        for v in range(PHASES):
            at = 16 * tile + ((v & 7) << 1) + (v >> 3)
            out_ref[:, at * LANES : (at + 1) * LANES] = mixed[v]


def shards(strain, filters, recon_weights, row_spans, slice_rates, delays, antenna):
    slice_index = lax.axis_index("cuts")
    slices = lax.axis_size("cuts")
    detector = lax.axis_index("det")
    detectors = lax.axis_size("det")
    bases, taps = filters.shape[1:]
    share = recon_weights.shape[1] // (slices * detectors)
    window = strain.shape[2] - taps
    tiles = strain.shape[2] // LANES
    place = jnp.stack([slice_index * detectors + detector, detector]).astype(jnp.int32)
    chunks = 4
    message = pl.pallas_call(
        compose,
        out_shape=jax.ShapeDtypeStruct((slices, taps // LANES * share + tiles, LANES), jnp.float32),
        in_specs=[
            pl.BlockSpec(memory_space=pltpu.SMEM),
            pl.BlockSpec(memory_space=pltpu.HBM),
            pl.BlockSpec(memory_space=pltpu.HBM),
            pl.BlockSpec(memory_space=pltpu.VMEM),
        ],
        out_specs=pl.BlockSpec(memory_space=pltpu.VMEM),
        scratch_shapes=[
            pltpu.VMEM((slices, share, bases), jnp.bfloat16),
            pltpu.VMEM((chunks, bases, taps // chunks), jnp.bfloat16),
            pltpu.SemaphoreType.DMA,
            pltpu.SemaphoreType.DMA((chunks,)),
        ],
        compiler_params=pltpu.CompilerParams(vmem_limit_bytes=32 * 1024 * 1024),
    )(place, recon_weights.reshape(slices, detectors, share, bases), filters, strain.reshape(tiles, LANES))
    received = lax.all_to_all(message, "cuts", split_axis=0, concat_axis=0, tiled=True)
    body = taps // LANES * share
    partner = lax.ppermute(received[:, body:], "det", [(0, 1), (1, 0)])
    depth = taps + BLOCK
    return pl.pallas_call(
        kernel,
        out_shape=jax.ShapeDtypeStruct((share, window), jnp.float32),
        in_specs=[pl.BlockSpec(memory_space=pltpu.SMEM)] * 5 + [pl.BlockSpec(memory_space=pltpu.VMEM)] * 2,
        out_specs=pl.BlockSpec(memory_space=pltpu.VMEM),
        scratch_shapes=[
            pltpu.VMEM((PHASES * share, SLOTS * depth), jnp.bfloat16),
            pltpu.VMEM((SLOTS, detectors, tiles // 2, 16, BLOCK), jnp.bfloat16),
            pltpu.VMEM((PHASES * share, detectors * 256), jnp.float32),
            pltpu.VMEM((PHASES * share, detectors * 128), jnp.float32),
            pltpu.VMEM((2, PHASES * share, detectors * 64), jnp.float32),
            pltpu.VMEM((detectors, 4 * PHASES, share, 256), jnp.float32),
        ],
        compiler_params=pltpu.CompilerParams(vmem_limit_bytes=32 * 1024 * 1024),
    )(slice_rates, row_spans, delays, antenna, place, received, partner)


def solution(mesh):
    placed = (
        P("cuts", "det", None),
        P(("bank", "cuts"), None, None),
        P(("bank", "cuts"), None, None),
        P("bank"),
        P(),
        P(),
        P(),
    )
    return jax.shard_map(
        shards,
        mesh=mesh,
        in_specs=placed,
        out_specs=P(("bank", "cuts", "det"), None),
        check_vma=False,
    )
```

time: 739 us -> 63.5 us (0.09)
  loops' own time: 253 us -> 0 us
  local copies, waits for them, and re-layouts: 221 us -> 2.41 us
  other arithmetic: 112 us -> 0.88 us
  waiting for transfers between devices: 92.6 us -> 1.15 us
  matrix products: 34.5 us -> 0 us
  blocking collectives: 5.93 us -> 38.5 us
  Pallas kernels: 0 us -> 17.3 us
  between operations: 14.2 us -> 0.06 us
    another operation x2 -> x0, loops' own time: 253 us -> none  [the longest x1 253 us: coherent(): lax.fori_loop(0, delays.shape[0], direction, jnp.zeros((height, window),...]
    max x64 -> x0, other arithmetic: 101 us -> none  [direction(): return jnp.maximum(highest, jnp.abs(summed))]
    unnamed x2 -> x0, waiting for transfers between devices: 92.6 us -> none
    dynamic_slice x137 -> x0, local copies, waits for them, and re-layouts: 86 us -> none  [the longest x64 42.1 us: direction(): summed = summed + antenna[number, detector] * shifted]
    reshape x9 -> x0, local copies, waits for them, and re-layouts: 45.1 us -> none  [the longest x8 44.2 us: hankel_block(): tiled.reshape(block_rows, length - 1)]
    another operation x16 -> x0, local copies, waits for them, and re-layouts: 38 us -> none  [hankel_block(): tiled = jnp.tile(backward, block_rows + 1)[:block_rows * (length - 1)]]
    dot_general x9 -> x0, matrix products: 34.5 us -> none  [the longest x8 28.3 us: one_block(): jnp.einsum('bt,it->bi', taps_bank, toeplitz, preferred_element_type=jnp.f...]
    all_to_all x1, blocking collectives: 5.93 us -> 38.5 us  [shards(): lax.all_to_all(message, 'cuts', split_axis=0, concat_axis=0, tiled=True)]
where the time goes in v3:
time: 63.5 us; the launch traced here: 62.6 us
  blocking collectives  38.5 us (61%)
  Pallas kernels  17.3 us (27%)
  local copies, waits for them, and re-layouts  2.41 us (4%)
  starting transfers between devices  2.39 us (4%)
  waiting for transfers between devices  1.15 us (2%)
  other arithmetic  0.88 us (1%)
    all_to_all x1, blocking collectives, shards(): lax.all_to_all(message, 'cuts', split_axis=0, concat_axis=0, tiled=True)  38.5 us
    pallas_call x1, Pallas kernels, shards(): pl.pallas_call(kernel, out_shape=jax.ShapeDtypeStruct((share, window), jn...  15.5 us
    ppermute x1, starting transfers between devices, shards(): partner = lax.ppermute(received[:, body:], 'det', [(0, 1), (1, 0)])  2.39 us
    unnamed x14, local copies, waits for them, and re-layouts  2.39 us
    pallas_call x1, Pallas kernels, shards(): pl.pallas_call(compose, out_shape=jax.ShapeDtypeStruct((slices, taps // L...  1.78 us
  transfers between devices with their start and end apart: 1, of which 1 were waited for; matrix products, arithmetic and copies ran while one was open for 0% of the time, Pallas kernels for 0%

profile of v3, /device:TPU:1, one launch (start us, length us, event | category | flops | bytes accessed | tf_op | source)
XLA Modules:
  0.0 62.6 jit_solution(15090064117783410158)
XLA Ops:
  0.0 0.1 pad_add_fusion.place
  0.1 0.8 %reduce = bf16[6144]{0:T(1024)(128)(2,1)S(1)} reduce(bf16[1,1,6144]{2,1,0:T(2,128)(2,1)} %param.7, bf16[]{:T(256)} %constant.16), dimensions={0,1}, to_apply=%param.7.reduce_sub_computation | reduce | bytes 24578 | tf_op args[0]
  0.9 0.0 copy-start
  0.9 1.2 %copy-done = bf16[1,256,2048]{2,1,0:T(8,128)(2,1)S(1)} copy-done((bf16[1,256,2048]{2,1,0:T(8,128)(2,1)S(1)}, bf16[1,256,2048]{2,1,0:T(8,128)(2,1)}, u32[]{:S(2)}) %copy-start) | copy-done | bytes 1048600
  2.1 0.0 copy-start.1
  2.1 0.9 %copy-done.1 = bf16[1,512,256]{2,1,0:T(8,128)(2,1)S(1)} copy-done((bf16[1,512,256]{2,1,0:T(8,128)(2,1)S(1)}, bf16[1,512,256]{2,1,0:T(8,128)(2,1)}, u32[]{:S(2)}) %copy-start.1) | copy-done | bytes 262168
  3.1 1.8 %shard_map.73 = f32[16,304,128]{2,1,0:T(8,128)S(1)} custom-call(s32[2]{0:T(128)S(1)} %pad_add_fusion.place, bf16[16,2,16,256]{3,2,1,0:T(8,128)(2,1)S(1)} %bitcast.4, bf16[1,256,2048]{2,1,0:T(8,128)(2,1)S(1)} %copy-done, bf16[48,128]{1,0:T(8,128)(2,1)S(1)} %bitcast.5), custom_call_target="tpu_custom_call" | custom-call | tf_op jit(solution)/shard_map/pallas_call | solution.py:223
  4.8 0.0 copy-start.4
  4.9 0.0 copy-start.5
  4.9 0.0 copy-start.2
  4.9 0.0 copy-start.3
  4.9 38.5 %all_to_all.5.g_ref = f32[16,304,128]{2,1,0:T(8,128)S(1)} all-to-all(f32[16,304,128]{2,1,0:T(8,128)S(1)} %shard_map.73), channel_id=1, replica_groups=mesh['cuts'=16,'det'=2,'bank'=8] {'cuts'}, dimensions={0} | all-to-all | bytes 4980736 | tf_op jit(solution)/shard_map/all_to_all | solution.py:241
  43.4 2.4 %collective-permute-start = (f32[16,48,128]{2,1,0:T(8,128)S(1)}, f32[16,48,128]{2,1,0:T(8,128)S(1)}, u32[]{:S(2)}, u32[]{:S(2)}) collective-permute-start(f32[16,48,128]{2,1,0:T(8,128)S(1)} %slice.4), channel_id=1, source_target_pairs={{0,8},{8,0},{1,9},{9,1},{2,10},{10,2},{3,11},{11,3},{4,12},{12,4},... | collective-permute-start | bytes 1179656 | tf_op jit(solution)/shard_map/ppermute | solution.py:243
  45.8 0.0 copy-done.4
  45.8 0.1 copy.8.delays
  45.9 0.0 copy-done.5
  45.9 0.1 copy.9.antenna
  46.0 1.2 %collective-permute-done.other_ref = f32[16,48,128]{2,1,0:T(8,128)S(1)} collective-permute-done((f32[16,48,128]{2,1,0:T(8,128)S(1)}, f32[16,48,128]{2,1,0:T(8,128)S(1)}, u32[]{:S(2)}, u32[]{:S(2)}) %collective-permute-start) | collective-permute-done | bytes 393248 | tf_op jit(solution)/shard_map/ppermute | solution.py:243
  47.1 0.0 copy-done.2
  47.1 0.0 copy-done.3
  47.1 15.5 %shard_map.74 = f32[16,4096]{1,0:T(8,128)} custom-call(s32[16]{0:T(128)S(1)} %copy-done.3, s32[512]{0:T(512)S(1)} %copy-done.2, s32[64,2]{1,0:T(8,128)S(1)} %copy.8.delays, f32[64,2]{1,0:T(8,128)S(1)} %copy.9.antenna, s32[2]{0:T(128)S(1)} %pad_add_fusion.place, f32[16,304,128]{2,1,0:T(8,128)S(1)} %all_to_all.5.g_ref, ...), custom_call_target="tpu_custom_call" | custom-call | tf_op jit(solution)/shard_map/pallas_call | solution.py:245
  (1 shorter events, 0.0 us)
Async XLA Ops:
  0.9 1.2 %copy-start = (bf16[1,256,2048]{2,1,0:T(8,128)(2,1)S(1)}, bf16[1,256,2048]{2,1,0:T(8,128)(2,1)}, u32[]{:S(2)}) copy-start(bf16[1,256,2048]{2,1,0:T(8,128)(2,1)} %filters_ref.1) | copy-start | bytes 3145732
  2.1 0.9 %copy-start.1 = (bf16[1,512,256]{2,1,0:T(8,128)(2,1)S(1)}, bf16[1,512,256]{2,1,0:T(8,128)(2,1)}, u32[]{:S(2)}) copy-start(bf16[1,512,256]{2,1,0:T(8,128)(2,1)} %param.9) | copy-start | bytes 786436
  4.8 40.9 %copy-start.4 = (s32[64,2]{0,1:T(2,128)S(1)}, s32[64,2]{0,1:T(2,128)}, u32[]{:S(2)}) copy-start(s32[64,2]{0,1:T(2,128)} %param.12) | copy-start | bytes 1540
  4.9 41.0 %copy-start.5 = (f32[64,2]{0,1:T(2,128)S(1)}, f32[64,2]{0,1:T(2,128)}, u32[]{:S(2)}) copy-start(f32[64,2]{0,1:T(2,128)} %param.13) | copy-start | bytes 1540
  4.9 42.2 %copy-start.2 = (s32[512]{0:T(512)S(1)}, s32[512]{0:T(512)}, u32[]{:S(2)}) copy-start(s32[512]{0:T(512)} %spans.1) | copy-start | bytes 6148
  4.9 42.2 %copy-start.3 = (s32[16]{0:T(128)S(1)}, s32[16]{0:T(128)}, u32[]{:S(2)}) copy-start(s32[16]{0:T(128)} %rates.1) | copy-start | bytes 196
  43.4 3.7 %collective-permute-start = (f32[16,48,128]{2,1,0:T(8,128)S(1)}, f32[16,48,128]{2,1,0:T(8,128)S(1)}, u32[]{:S(2)}, u32[]{:S(2)}) collective-permute-start(f32[16,48,128]{2,1,0:T(8,128)S(1)} %slice.4), channel_id=1, source_target_pairs={{0,8},{8,0},{1,9},{9,1},{2,10},{10,2},{3,11},{11,3},{4,12},{12,4},... | collective-permute-start | bytes 1179656 | tf_op jit(solution)/shard_map/ppermute | solution.py:243

commit v4 on v3

--- a/solution.py
+++ b/solution.py
@@ -11,21 +11,10 @@
 SLOTS = 4
 
 
-def compose(place, weights_ref, filters_ref, strain_ref, out_ref, weights, filters, got, arrived):
-    chunks, _, width = filters.shape
-    targets, share, bases = weights.shape
-    here = pltpu.make_async_copy(weights_ref.at[:, place[1]], weights, got)
-    here.start()
-    parts = [
-        pltpu.make_async_copy(
-            filters_ref.at[0, :, chunk * width : (chunk + 1) * width], filters.at[chunk], arrived.at[chunk]
-        )
-        for chunk in range(chunks)
-    ]
-    for part in parts:
-        part.start()
-    end = out_ref.shape[1]
-    count = strain_ref.shape[0]
+def compose(place, weights_ref, filters_ref, strain_ref, out_ref):
+    targets, _, share, bases = weights_ref.shape
+    taps, width = filters_ref.shape[2], 4 * LANES
+    end, count = out_ref.shape[1], strain_ref.shape[0]
     flip = (
         lax.broadcasted_iota(jnp.int32, (LANES, LANES), 0) + lax.broadcasted_iota(jnp.int32, (LANES, LANES), 1)
         == LANES - 1
@@ -33,11 +22,10 @@
     backward = jnp.dot(strain_ref[...], flip, preferred_element_type=jnp.float32)
     for target in range(targets):
         out_ref[target, end - count : end, :] = backward
-    here.wait()
-    for chunk, part in enumerate(parts):
-        part.wait()
+    weights = weights_ref[:, place[1]].reshape(targets * share, bases)
+    for chunk in range(taps // width):
         rows = jnp.dot(
-            weights[...].reshape(targets * share, bases), filters[chunk], preferred_element_type=jnp.float32
+            weights, filters_ref[0, :, chunk * width : (chunk + 1) * width], preferred_element_type=jnp.float32
         )
         for tile in range(width // LANES):
             at = chunk * width // LANES + tile
@@ -196,7 +184,7 @@
             return jnp.maximum(highest, jnp.abs(one + two))
 
         highest = lax.fori_loop(
-            0, directions, direction, jnp.zeros((group, rows, 2 * LANES), jnp.float32), unroll=8
+            0, directions, direction, jnp.zeros((group, rows, 2 * LANES), jnp.float32), unroll=32
         )
         for p in range(group):
             full[(start + p) * rows : (start + p + 1) * rows, 0 : 2 * LANES] = highest[p]
@@ -219,23 +207,11 @@
     window = strain.shape[2] - taps
     tiles = strain.shape[2] // LANES
     place = jnp.stack([slice_index * detectors + detector, detector]).astype(jnp.int32)
-    chunks = 4
     message = pl.pallas_call(
         compose,
         out_shape=jax.ShapeDtypeStruct((slices, taps // LANES * share + tiles, LANES), jnp.float32),
-        in_specs=[
-            pl.BlockSpec(memory_space=pltpu.SMEM),
-            pl.BlockSpec(memory_space=pltpu.HBM),
-            pl.BlockSpec(memory_space=pltpu.HBM),
-            pl.BlockSpec(memory_space=pltpu.VMEM),
-        ],
+        in_specs=[pl.BlockSpec(memory_space=pltpu.SMEM)] + [pl.BlockSpec(memory_space=pltpu.VMEM)] * 3,
         out_specs=pl.BlockSpec(memory_space=pltpu.VMEM),
-        scratch_shapes=[
-            pltpu.VMEM((slices, share, bases), jnp.bfloat16),
-            pltpu.VMEM((chunks, bases, taps // chunks), jnp.bfloat16),
-            pltpu.SemaphoreType.DMA,
-            pltpu.SemaphoreType.DMA((chunks,)),
-        ],
         compiler_params=pltpu.CompilerParams(vmem_limit_bytes=32 * 1024 * 1024),
     )(place, recon_weights.reshape(slices, detectors, share, bases), filters, strain.reshape(tiles, LANES))
     received = lax.all_to_all(message, "cuts", split_axis=0, concat_axis=0, tiled=True)

time: 63.5 us -> 63.1 us (level)
    pallas_call x1, Pallas kernels: 1.78 us -> 0.98 us  [shards(): pl.pallas_call(compose, out_shape=jax.ShapeDtypeStruct((slices, taps // L...]
where the time goes in v4:
time: 63.1 us; the launch traced here: 62.3 us
  blocking collectives  38.4 us (61%)
  Pallas kernels  16.9 us (27%)
  local copies, waits for them, and re-layouts  2.41 us (4%)
  starting transfers between devices  2.41 us (4%)
  waiting for transfers between devices  1.15 us (2%)
  other arithmetic  0.88 us (1%)
    all_to_all x1, blocking collectives, shards(): lax.all_to_all(message, 'cuts', split_axis=0, concat_axis=0, tiled=True)  38.4 us
    pallas_call x1, Pallas kernels, shards(): pl.pallas_call(kernel, out_shape=jax.ShapeDtypeStruct((share, window), jn...  15.9 us
    ppermute x1, starting transfers between devices, shards(): partner = lax.ppermute(received[:, body:], 'det', [(0, 1), (1, 0)])  2.41 us
    unnamed x14, local copies, waits for them, and re-layouts  2.39 us
  transfers between devices with their start and end apart: 1, of which 1 were waited for; matrix products, arithmetic and copies ran while one was open for 0% of the time, Pallas kernels for 0%

profile of v4, /device:TPU:1, one launch (start us, length us, event | category | flops | bytes accessed | tf_op | source)
XLA Modules:
  0.0 62.3 jit_solution(2064096619157882475)
XLA Ops:
  0.0 0.1 pad_add_fusion.place
  0.1 0.8 %reduce = bf16[6144]{0:T(1024)(128)(2,1)S(1)} reduce(bf16[1,1,6144]{2,1,0:T(2,128)(2,1)} %param.7, bf16[]{:T(256)} %constant.16), dimensions={0,1}, to_apply=%param.7.reduce_sub_computation | reduce | bytes 24578 | tf_op args[0]
  0.9 0.0 copy-start
  0.9 1.2 %copy-done = bf16[1,256,2048]{2,1,0:T(8,128)(2,1)S(1)} copy-done((bf16[1,256,2048]{2,1,0:T(8,128)(2,1)S(1)}, bf16[1,256,2048]{2,1,0:T(8,128)(2,1)}, u32[]{:S(2)}) %copy-start) | copy-done | bytes 1048600
  2.1 0.0 copy-start.1
  2.1 0.9 %copy-done.1 = bf16[1,512,256]{2,1,0:T(8,128)(2,1)S(1)} copy-done((bf16[1,512,256]{2,1,0:T(8,128)(2,1)S(1)}, bf16[1,512,256]{2,1,0:T(8,128)(2,1)}, u32[]{:S(2)}) %copy-start.1) | copy-done | bytes 262168
  3.1 1.0 %shard_map.73 = f32[16,304,128]{2,1,0:T(8,128)S(1)} custom-call(s32[2]{0:T(128)S(1)} %pad_add_fusion.place, bf16[16,2,16,256]{3,2,1,0:T(8,128)(2,1)S(1)} %bitcast.4, bf16[1,256,2048]{2,1,0:T(8,128)(2,1)S(1)} %copy-done, bf16[48,128]{1,0:T(8,128)(2,1)S(1)} %bitcast.5), custom_call_target="tpu_custom_call" | custom-call | tf_op jit(solution)/shard_map/pallas_call | solution.py:210
  4.0 0.0 copy-start.4
  4.1 0.0 copy-start.5
  4.1 0.0 copy-start.2
  4.1 0.0 copy-start.3
  4.1 38.4 %all_to_all.5.g_ref = f32[16,304,128]{2,1,0:T(8,128)S(1)} all-to-all(f32[16,304,128]{2,1,0:T(8,128)S(1)} %shard_map.73), channel_id=1, replica_groups=mesh['cuts'=16,'det'=2,'bank'=8] {'cuts'}, dimensions={0} | all-to-all | bytes 4980736 | tf_op jit(solution)/shard_map/all_to_all | solution.py:217
  42.6 2.4 %collective-permute-start = (f32[16,48,128]{2,1,0:T(8,128)S(1)}, f32[16,48,128]{2,1,0:T(8,128)S(1)}, u32[]{:S(2)}, u32[]{:S(2)}) collective-permute-start(f32[16,48,128]{2,1,0:T(8,128)S(1)} %slice.4), channel_id=1, source_target_pairs={{0,8},{8,0},{1,9},{9,1},{2,10},{10,2},{3,11},{11,3},{4,12},{12,4},... | collective-permute-start | bytes 1179656 | tf_op jit(solution)/shard_map/ppermute | solution.py:219
  45.0 0.0 copy-done.4
  45.0 0.1 copy.8.delays
  45.1 0.0 copy-done.5
  45.1 0.1 copy.9.antenna
  45.2 1.2 %collective-permute-done.other_ref = f32[16,48,128]{2,1,0:T(8,128)S(1)} collective-permute-done((f32[16,48,128]{2,1,0:T(8,128)S(1)}, f32[16,48,128]{2,1,0:T(8,128)S(1)}, u32[]{:S(2)}, u32[]{:S(2)}) %collective-permute-start) | collective-permute-done | bytes 393248 | tf_op jit(solution)/shard_map/ppermute | solution.py:219
  46.3 0.0 copy-done.2
  46.3 0.0 copy-done.3
  46.3 15.9 %shard_map.74 = f32[16,4096]{1,0:T(8,128)} custom-call(s32[16]{0:T(128)S(1)} %copy-done.3, s32[512]{0:T(512)S(1)} %copy-done.2, s32[64,2]{1,0:T(8,128)S(1)} %copy.8.delays, f32[64,2]{1,0:T(8,128)S(1)} %copy.9.antenna, s32[2]{0:T(128)S(1)} %pad_add_fusion.place, f32[16,304,128]{2,1,0:T(8,128)S(1)} %all_to_all.5.g_ref, ...), custom_call_target="tpu_custom_call" | custom-call | tf_op jit(solution)/shard_map/pallas_call | solution.py:221
  (1 shorter events, 0.0 us)
Async XLA Ops:
  0.9 1.2 %copy-start = (bf16[1,256,2048]{2,1,0:T(8,128)(2,1)S(1)}, bf16[1,256,2048]{2,1,0:T(8,128)(2,1)}, u32[]{:S(2)}) copy-start(bf16[1,256,2048]{2,1,0:T(8,128)(2,1)} %filters_ref.1) | copy-start | bytes 3145732
  2.1 0.9 %copy-start.1 = (bf16[1,512,256]{2,1,0:T(8,128)(2,1)S(1)}, bf16[1,512,256]{2,1,0:T(8,128)(2,1)}, u32[]{:S(2)}) copy-start(bf16[1,512,256]{2,1,0:T(8,128)(2,1)} %param.9) | copy-start | bytes 786436
  4.0 40.9 %copy-start.4 = (s32[64,2]{0,1:T(2,128)S(1)}, s32[64,2]{0,1:T(2,128)}, u32[]{:S(2)}) copy-start(s32[64,2]{0,1:T(2,128)} %param.12) | copy-start | bytes 1540
  4.1 41.0 %copy-start.5 = (f32[64,2]{0,1:T(2,128)S(1)}, f32[64,2]{0,1:T(2,128)}, u32[]{:S(2)}) copy-start(f32[64,2]{0,1:T(2,128)} %param.13) | copy-start | bytes 1540
  4.1 42.3 %copy-start.2 = (s32[512]{0:T(512)S(1)}, s32[512]{0:T(512)}, u32[]{:S(2)}) copy-start(s32[512]{0:T(512)} %spans.1) | copy-start | bytes 6148
  4.1 42.3 %copy-start.3 = (s32[16]{0:T(128)S(1)}, s32[16]{0:T(128)}, u32[]{:S(2)}) copy-start(s32[16]{0:T(128)} %rates.1) | copy-start | bytes 196
  42.6 3.8 %collective-permute-start = (f32[16,48,128]{2,1,0:T(8,128)S(1)}, f32[16,48,128]{2,1,0:T(8,128)S(1)}, u32[]{:S(2)}, u32[]{:S(2)}) collective-permute-start(f32[16,48,128]{2,1,0:T(8,128)S(1)} %slice.4), channel_id=1, source_target_pairs={{0,8},{8,0},{1,9},{9,1},{2,10},{10,2},{3,11},{11,3},{4,12},{12,4},... | collective-permute-start | bytes 1179656 | tf_op jit(solution)/shard_map/ppermute | solution.py:219
